TPU v7x, 512 devices: a whole 4x8x8 slice. The times are simulated.
512 devices in a mesh: wide: 64 (over z, y_lo, core), narrow: 8 (over y_hi, x).
Axes of the slice: x: 4, y: 8 (y_hi: 2, y_lo: 4; y = y_hi * 4 + y_lo), z: 8, core: 2. Of those that a mesh axis runs over, the one named last changes fastest.
Arguments:
- volume: float32 [256, 128, 1024], P('wide', 'narrow'), may hold values from -12 to 12
Outputs:
- smoothed: float32 [256, 128, 1024], P('wide', 'narrow')
All inputs are finite; a program needn't handle non-finite values.
Results may differ from a plain program's by a relative error of at most 0.00019.
Values sent between devices are 32-bit elements; how exact they have to be, the bound alone decides.
No kernel may reach another device: no remote copies, remote signals or barrier semaphores. Data moves between devices by JAX's collectives and lax.ppermute only.
A program may use at most 64 MiB of HBM per device.

v0:
```python
import jax
import jax.numpy as jnp
from jax import lax
from jax.sharding import PartitionSpec as P

step_weight = 300.0
contrast_sq = 9.0


def with_halo(shard, sides, width):
    for axis, dim in sides:
        count, length = (lax.axis_size(axis), shard.shape[dim])
        up = [(i, (i + 1) % count) for i in range(count - 1)]
        down = [(j, i) for i, j in up]
        last = lax.slice_in_dim(shard, length - width, length, axis=dim)
        first = lax.slice_in_dim(shard, 0, width, axis=dim)
        before = lax.ppermute(last, axis, up)
        after = lax.ppermute(first, axis, down)
        shard = jnp.concatenate([before, shard, after], axis=dim)
    return shard


def cyclic_solve(lower, diag, upper, values):
    length = values.shape[0]
    if length == 1:
        return values / diag
    middle = length // 2

    def halves(field):
        paired = field.reshape((middle, 2) + field.shape[1:])
        return (paired[:, 0], paired[:, 1])

    def after(field, filler):
        return jnp.concatenate([field[1:], jnp.full_like(field[:1], filler)], 0)

    lower_even, lower_odd = halves(lower)
    diag_even, diag_odd = halves(diag)
    upper_even, upper_odd = halves(upper)
    value_even, value_odd = halves(values)
    factor_left = -lower_odd / diag_even
    factor_right = -upper_odd / after(diag_even, 1.0)
    odd_part = cyclic_solve(
        factor_left * lower_even,
        diag_odd + factor_left * upper_even + factor_right * after(lower_even, 0.0),
        factor_right * after(upper_even, 0.0),
        value_odd + factor_left * value_even + factor_right * after(value_even, 0.0),
    )
    previous = jnp.concatenate([jnp.zeros_like(odd_part[:1]), odd_part[:-1]], 0)
    even_part = (value_even - lower_even * previous - upper_even * odd_part) / diag_even
    return jnp.stack([even_part, odd_part], 1).reshape(values.shape)


def diffuse(values, cond):
    between = 0.5 * (cond[:-1] + cond[1:])
    edge = jnp.zeros_like(cond[:1])
    lower = jnp.concatenate([edge, -step_weight * between], 0)
    upper = jnp.concatenate([-step_weight * between, edge], 0)
    return cyclic_solve(lower, 1.0 - lower - upper, upper, values)


def per_device(volume):
    inl, crs, tms = volume.shape
    wide_count = lax.axis_size("wide")
    narrow_count = lax.axis_size("narrow")
    wide_rank = lax.axis_index("wide")
    narrow_rank = lax.axis_index("narrow")
    padded = with_halo(volume, (("wide", 0), ("narrow", 1)), 1)
    first_row = jnp.where(wide_rank == 0, padded[1:2], padded[0:1])
    final_row = jnp.where(wide_rank == wide_count - 1, padded[-2:-1], padded[-1:])
    padded = jnp.concatenate([first_row, padded[1:-1], final_row], 0)
    first_col = jnp.where(narrow_rank == 0, padded[:, 1:2], padded[:, 0:1])
    final_col = jnp.where(narrow_rank == narrow_count - 1, padded[:, -2:-1], padded[:, -1:])
    padded = jnp.concatenate([first_col, padded[:, 1:-1], final_col], 1)
    power = (0.5 * (padded[2:, 1:-1] - padded[:-2, 1:-1])) ** 2
    power = power + (0.5 * (padded[1:-1, 2:] - padded[1:-1, :-2])) ** 2
    timed = jnp.concatenate([volume[:, :, :1], volume, volume[:, :, -1:]], 2)
    power = power + (0.5 * (timed[:, :, 2:] - timed[:, :, :-2])) ** 2
    cond = 1.0 / (1.0 + power / contrast_sq)
    traces = inl * crs
    solved = diffuse(volume.reshape(traces, tms).T, cond.reshape(traces, tms).T)
    along_time = solved.T.reshape(inl, crs, tms)
    columns = crs * tms
    lines = (
        lax.all_to_all(
            volume.reshape(inl, columns), "wide", split_axis=1, concat_axis=0, tiled=True
        ),
        lax.all_to_all(cond.reshape(inl, columns), "wide", split_axis=1, concat_axis=0, tiled=True),
    )
    solved = diffuse(lines[0], lines[1])
    along_inline = lax.all_to_all(solved, "wide", split_axis=0, concat_axis=1, tiled=True).reshape(
        inl, crs, tms
    )
    lines = (
        lax.all_to_all(volume, "narrow", split_axis=2, concat_axis=1, tiled=True),
        lax.all_to_all(cond, "narrow", split_axis=2, concat_axis=1, tiled=True),
    )
    solved = diffuse(jnp.transpose(lines[0], (1, 0, 2)), jnp.transpose(lines[1], (1, 0, 2)))
    along_cross = lax.all_to_all(
        jnp.transpose(solved, (1, 0, 2)), "narrow", split_axis=1, concat_axis=2, tiled=True
    )
    lateral = along_inline + along_cross
    return (lateral + along_time) / 3.0


def solution(mesh):
    placed = (P("wide", "narrow", None),)
    return jax.shard_map(
        per_device, mesh=mesh, in_specs=placed, out_specs=P("wide", "narrow", None), check_vma=False
    )
```

profile of v0, /device:TPU:1, one launch (start us, length us, event | category | flops | bytes accessed | tf_op | source)
XLA Modules:
  0.0 156.7 jit_solution(9909950086737457264)
XLA Ops:
  0.0 0.9 fusion.175
  0.9 4.6 %collective-permute-start = (f32[1,16,1024]{2,1,0:T(8,128)S(1)}, f32[1,16,1024]{2,1,0:T(8,128)S(1)}, u32[]{:S(2)}, u32[]{:S(2)}) collective-permute-start(f32[1,16,1024]{2,1,0:T(8,128)S(1)} %get-tuple-element.81), channel_id=1, source_target_pairs={{0,8},{8,16},{16,24},{24,32},{32,40},{40,48},{48,56},{56,64},{64,7... | collective-permute-start | bytes 196616 | tf_op jit(solution)/shard_map/ppermute | solution.py:17
  5.5 5.6 %collective-permute-start.1 = (f32[1,16,1024]{2,1,0:T(8,128)S(1)}, f32[1,16,1024]{2,1,0:T(8,128)S(1)}, u32[]{:S(2)}, u32[]{:S(2)}) collective-permute-start(f32[1,16,1024]{2,1,0:T(8,128)S(1)} %get-tuple-element.80), channel_id=1, source_target_pairs={{8,0},{16,8},{24,16},{32,24},{40,32},{48,40},{56,48},{64,56},{72,6... | collective-permute-start | bytes 196616 | tf_op jit(solution)/shard_map/ppermute | solution.py:18
  11.1 1.7 %copy.1462 = f32[4,16,1024]{1,0,2:T(4,128)S(1)} copy(f32[4,16,1024]{2,1,0:T(8,128)} %param.1) | data formatting | bytes 524288 | tf_op args[0]
  12.8 2.3 %reshape.948 = f32[8,1,8192]{2,1,0:T(1,128)} reshape(f32[1024,4,16]{2,1,0:T(4,128)S(1)} %bitcast.1584) | data formatting | bytes 524288
  15.1 4.8 %all-to-all-start.3 = ((f32[8,1,8192]{2,1,0:T(1,128)}), f32[8,1,8192]{2,1,0:T(1,128)S(1)}, u32[]{:S(2)}, u32[]{:S(2)}) async-start(f32[8,1,8192]{2,1,0:T(1,128)} %reshape.948), calls=%async_computation.3 | async-start | bytes 524288 | tf_op jit(solution)/shard_map/all_to_all | solution.py:94
  20.1 1.1 fusion.156
  21.4 3.4 %collective-permute-start.2 = (f32[6,1,1024]{2,1,0:T(1,128)S(1)}, f32[6,1,1024]{2,1,0:T(1,128)S(1)}, u32[]{:S(2)}, u32[]{:S(2)}) collective-permute-start(f32[6,1,1024]{2,1,0:T(1,128)S(1)} %get-tuple-element.38), channel_id=1, source_target_pairs={{0,1},{1,2},{2,3},{3,4},{4,5},{5,6},{6,7},{8,9},{9,10},{10,11},{11... | collective-permute-start | bytes 73736 | tf_op jit(solution)/shard_map/ppermute | solution.py:17
  24.7 1.3 collective-permute-start.3
  26.4 0.9 copy.1373
  27.3 2.4 %collective-permute-done.3 = f32[6,1,1024]{2,1,0:T(1,128)S(1)} collective-permute-done((f32[6,1,1024]{2,1,0:T(1,128)S(1)}, f32[6,1,1024]{2,1,0:T(1,128)S(1)}, u32[]{:S(2)}, u32[]{:S(2)}) %collective-permute-start.3) | collective-permute-done | bytes 24608 | tf_op jit(solution)/shard_map/ppermute | solution.py:18
  30.9 1.1 fusion.157
  38.5 18.1 %all-to-all-start = ((f32[4,64,256]{2,0,1:T(4,128)}), f32[4,64,256]{2,0,1:T(4,128)}, u32[]{:S(2)}, u32[]{:S(2)}) async-start(f32[4,64,256]{2,0,1:T(4,128)} %copy.1373), calls=%async_computation | async-start | bytes 524288 | tf_op jit(solution)/shard_map/all_to_all | solution.py:84
  58.0 2.3 %reshape.946 = f32[8,1,8192]{2,1,0:T(1,128)} reshape(f32[1024,4,16]{2,1,0:T(4,128)S(1)} %bitcast.1585) | data formatting | bytes 524288
  62.0 8.0 %all-to-all-done = f32[4,64,256]{2,0,1:T(4,128)} async-done(((f32[4,64,256]{2,0,1:T(4,128)}), f32[4,64,256]{2,0,1:T(4,128)}, u32[]{:S(2)}, u32[]{:S(2)}) %all-to-all-start) | async-done | bytes 262176 | tf_op jit(solution)/shard_map/all_to_all | solution.py:84
  70.0 13.6 %all-to-all-start.4 = ((f32[8,1,8192]{2,1,0:T(1,128)}), f32[8,1,8192]{2,1,0:T(1,128)}, u32[]{:S(2)}, u32[]{:S(2)}) async-start(f32[8,1,8192]{2,1,0:T(1,128)} %reshape.946), calls=%async_computation.4 | async-start | bytes 524288 | tf_op jit(solution)/shard_map/all_to_all | solution.py:95
  83.6 1.0 subtract_divide_fusion.2
  84.6 0.9 copy.1375
  87.0 1.3 reduce.1
  88.3 1.5 reshape.949
  91.3 0.9 fusion.163
  92.2 1.2 reshape.840
  94.2 7.3 %all-to-all-start.1 = ((f32[4,64,256]{2,0,1:T(4,128)}), f32[4,64,256]{2,0,1:T(4,128)}, u32[]{:S(2)}, u32[]{:S(2)}) async-start(f32[4,64,256]{2,0,1:T(4,128)} %copy.1375), calls=%async_computation.1 | async-start | bytes 524288 | tf_op jit(solution)/shard_map/all_to_all | solution.py:87
  101.5 2.3 %reduce = f32[8,8192]{1,0:T(8,128)S(1)} reduce(f32[8,1,8192]{2,1,0:T(1,128)} %all-to-all-done.4, f32[]{:T(128)} %broadcast.298), dimensions={1}, to_apply=%all_to_all.91.reduce_sub_computation | reduce | bytes 524292 | tf_op jit(solution)/shard_map/all_to_all | solution.py:95
  103.7 1.5 reshape.947
  110.7 4.2 %all-to-all-done.1 = f32[4,64,256]{2,0,1:T(4,128)} async-done(((f32[4,64,256]{2,0,1:T(4,128)}), f32[4,64,256]{2,0,1:T(4,128)}, u32[]{:S(2)}, u32[]{:S(2)}) %all-to-all-start.1) | async-done | bytes 262176 | tf_op jit(solution)/shard_map/all_to_all | solution.py:87
  114.9 7.8 %all-to-all-start.5 = ((f32[4,128,128]{2,0,1:T(4,128)}), f32[4,128,128]{2,0,1:T(4,128)S(1)}, u32[]{:S(2)}, u32[]{:S(2)}) async-start(f32[4,128,128]{2,0,1:T(4,128)} %copy.1542), calls=%async_computation.5 | async-start | bytes 524288 | tf_op jit(solution)/shard_map/all_to_all | solution.py:98
  122.7 1.0 all_to_all.83
  130.0 0.9 all_to_all.84
  130.9 1.8 %all-to-all-done.5 = f32[4,128,128]{2,0,1:T(4,128)S(1)} async-done(((f32[4,128,128]{2,0,1:T(4,128)}), f32[4,128,128]{2,0,1:T(4,128)S(1)}, u32[]{:S(2)}, u32[]{:S(2)}) %all-to-all-start.5) | async-done | bytes 262176 | tf_op jit(solution)/shard_map/all_to_all | solution.py:98
  132.8 9.6 %all-to-all-start.2 = ((f32[64,4,256]{2,1,0:T(4,128)}), f32[64,4,256]{2,1,0:T(4,128)S(1)}, u32[]{:S(2)}, u32[]{:S(2)}) async-start(f32[64,4,256]{2,1,0:T(4,128)} %all_to_all.84), calls=%async_computation.2 | async-start | bytes 524288 | tf_op jit(solution)/shard_map/all_to_all | solution.py:90
  143.6 12.3 %all-to-all-done.2 = f32[64,4,256]{2,1,0:T(4,128)S(1)} async-done(((f32[64,4,256]{2,1,0:T(4,128)}), f32[64,4,256]{2,1,0:T(4,128)S(1)}, u32[]{:S(2)}, u32[]{:S(2)}) %all-to-all-start.2) | async-done | bytes 262176 | tf_op jit(solution)/shard_map/all_to_all | solution.py:90
  (474 shorter events, 26.0 us)
Async XLA Ops:
  0.9 20.4 %collective-permute-start = (f32[1,16,1024]{2,1,0:T(8,128)S(1)}, f32[1,16,1024]{2,1,0:T(8,128)S(1)}, u32[]{:S(2)}, u32[]{:S(2)}) collective-permute-start(f32[1,16,1024]{2,1,0:T(8,128)S(1)} %get-tuple-element.81), channel_id=1, source_target_pairs={{0,8},{8,16},{16,24},{24,32},{32,40},{40,48},{48,56},{56,64},{64,7... | collective-permute-start | bytes 196616 | tf_op jit(solution)/shard_map/ppermute | solution.py:17
  5.5 14.4 %copy-start = (f32[4,16,1024]{2,1,0:T(8,128)S(1)}, f32[4,16,1024]{2,1,0:T(8,128)}, u32[]{:S(2)}) copy-start(f32[4,16,1024]{2,1,0:T(8,128)} %param.1) | copy-start | bytes 786436
  5.5 15.8 %collective-permute-start.1 = (f32[1,16,1024]{2,1,0:T(8,128)S(1)}, f32[1,16,1024]{2,1,0:T(8,128)S(1)}, u32[]{:S(2)}, u32[]{:S(2)}) collective-permute-start(f32[1,16,1024]{2,1,0:T(8,128)S(1)} %get-tuple-element.80), channel_id=1, source_target_pairs={{8,0},{16,8},{24,16},{32,24},{40,32},{48,40},{56,48},{64,56},{72,6... | collective-permute-start | bytes 196616 | tf_op jit(solution)/shard_map/ppermute | solution.py:18
  15.1 23.3 %all-to-all-start.3 = ((f32[8,1,8192]{2,1,0:T(1,128)}), f32[8,1,8192]{2,1,0:T(1,128)S(1)}, u32[]{:S(2)}, u32[]{:S(2)}) async-start(f32[8,1,8192]{2,1,0:T(1,128)} %reshape.948), calls=%async_computation.3 | async-start | bytes 524288 | tf_op jit(solution)/shard_map/all_to_all | solution.py:94
  21.4 5.9 %collective-permute-start.2 = (f32[6,1,1024]{2,1,0:T(1,128)S(1)}, f32[6,1,1024]{2,1,0:T(1,128)S(1)}, u32[]{:S(2)}, u32[]{:S(2)}) collective-permute-start(f32[6,1,1024]{2,1,0:T(1,128)S(1)} %get-tuple-element.38), channel_id=1, source_target_pairs={{0,1},{1,2},{2,3},{3,4},{4,5},{5,6},{6,7},{8,9},{9,10},{10,11},{11... | collective-permute-start | bytes 73736 | tf_op jit(solution)/shard_map/ppermute | solution.py:17
  24.7 4.9 %collective-permute-start.3 = (f32[6,1,1024]{2,1,0:T(1,128)S(1)}, f32[6,1,1024]{2,1,0:T(1,128)S(1)}, u32[]{:S(2)}, u32[]{:S(2)}) collective-permute-start(f32[6,1,1024]{2,1,0:T(1,128)S(1)} %get-tuple-element.39), channel_id=1, source_target_pairs={{1,0},{2,1},{3,2},{4,3},{5,4},{6,5},{7,6},{9,8},{10,9},{11,10},{12... | collective-permute-start | bytes 73736 | tf_op jit(solution)/shard_map/ppermute | solution.py:18
  33.0 1.0 copy-start.12
  34.4 1.2 copy-start.4
  35.8 1.2 copy-start.16
  36.0 1.1 copy-start.13
  36.4 1.1 copy-start.18
  36.6 1.8 %copy-start.23 = (f32[64,1,64]{2,1,0:T(1,128)}, f32[64,1,64]{2,1,0:T(1,128)S(1)}, u32[]{:S(2)}) copy-start(f32[64,1,64]{2,1,0:T(1,128)S(1)} %get-tuple-element.144) | copy-start | bytes 49156
  36.7 1.7 %copy-start.20 = (f32[64,1,64]{2,1,0:T(1,128)}, f32[64,1,64]{2,1,0:T(1,128)S(1)}, u32[]{:S(2)}) copy-start(f32[64,1,64]{2,1,0:T(1,128)S(1)} %get-tuple-element.146) | copy-start | bytes 49156
  36.8 19.7 %copy-start.24 = (f32[64,1,64]{2,1,0:T(1,128)}, f32[64,1,64]{2,1,0:T(1,128)S(1)}, u32[]{:S(2)}) copy-start(f32[64,1,64]{2,1,0:T(1,128)S(1)} %get-tuple-element.141) | copy-start | bytes 49156
  37.0 19.6 %copy-start.25 = (f32[64,1,64]{2,1,0:T(1,128)}, f32[64,1,64]{2,1,0:T(1,128)S(1)}, u32[]{:S(2)}) copy-start(f32[64,1,64]{2,1,0:T(1,128)S(1)} %get-tuple-element.148) | copy-start | bytes 49156
  38.4 18.1 %copy-start.14 = (f32[8,1,8192]{2,1,0:T(1,128)}, f32[8,1,8192]{2,1,0:T(1,128)S(1)}, u32[]{:S(2)}) copy-start(f32[8,1,8192]{2,1,0:T(1,128)S(1)} %all-to-all-done.3) | copy-start | bytes 786436
  38.5 31.5 %all-to-all-start = ((f32[4,64,256]{2,0,1:T(4,128)}), f32[4,64,256]{2,0,1:T(4,128)}, u32[]{:S(2)}, u32[]{:S(2)}) async-start(f32[4,64,256]{2,0,1:T(4,128)} %copy.1373), calls=%async_computation | async-start | bytes 524288 | tf_op jit(solution)/shard_map/all_to_all | solution.py:84
  60.3 26.7 %copy-start.15 = (f32[8,1,8192]{2,1,0:T(1,128)S(1)}, f32[8,1,8192]{2,1,0:T(1,128)}, u32[]{:S(2)}) copy-start(f32[8,1,8192]{2,1,0:T(1,128)} %copy-done.14) | copy-start | bytes 786436
  70.0 24.2 %all-to-all-start.4 = ((f32[8,1,8192]{2,1,0:T(1,128)}), f32[8,1,8192]{2,1,0:T(1,128)}, u32[]{:S(2)}, u32[]{:S(2)}) async-start(f32[8,1,8192]{2,1,0:T(1,128)} %reshape.946), calls=%async_computation.4 | async-start | bytes 524288 | tf_op jit(solution)/shard_map/all_to_all | solution.py:95
  93.4 8.1 %copy-start.2 = (f32[128,2,256]{2,1,0:T(2,128)}, f32[128,2,256]{2,1,0:T(2,128)S(1)}, u32[]{:S(2)}) copy-start(f32[128,2,256]{2,1,0:T(2,128)S(1)} %reshape.840) | copy-start | bytes 786436
  94.2 20.7 %all-to-all-start.1 = ((f32[4,64,256]{2,0,1:T(4,128)}), f32[4,64,256]{2,0,1:T(4,128)}, u32[]{:S(2)}, u32[]{:S(2)}) async-start(f32[4,64,256]{2,0,1:T(4,128)} %copy.1375), calls=%async_computation.1 | async-start | bytes 524288 | tf_op jit(solution)/shard_map/all_to_all | solution.py:87
  106.0 1.1 copy-start.22
  106.0 1.2 copy-start.8
  106.1 1.2 copy-start.19
  109.8 14.3 %copy-start.3 = (f32[128,2,256]{2,1,0:T(2,128)S(1)}, f32[128,2,256]{2,1,0:T(2,128)}, u32[]{:S(2)}) copy-start(f32[128,2,256]{2,1,0:T(2,128)} %copy-done.2) | copy-start | bytes 786436
  114.9 17.9 %all-to-all-start.5 = ((f32[4,128,128]{2,0,1:T(4,128)}), f32[4,128,128]{2,0,1:T(4,128)S(1)}, u32[]{:S(2)}, u32[]{:S(2)}) async-start(f32[4,128,128]{2,0,1:T(4,128)} %copy.1542), calls=%async_computation.5 | async-start | bytes 524288 | tf_op jit(solution)/shard_map/all_to_all | solution.py:98
  124.1 1.4 copy-start.21
  129.3 13.0 %copy-start.1 = (f32[128,2,64]{2,1,0:T(2,128)S(1)}, f32[128,2,64]{2,1,0:T(2,128)}, u32[]{:S(2)}) copy-start(f32[128,2,64]{2,1,0:T(2,128)} %copy.1654) | copy-start | bytes 196612
  129.3 13.0 %copy-start.5 = (f32[256,1,64]{2,1,0:T(1,128)S(1)}, f32[256,1,64]{2,1,0:T(1,128)}, u32[]{:S(2)}) copy-start(f32[256,1,64]{2,1,0:T(1,128)} %copy-done.4) | copy-start | bytes 196612
  129.3 13.0 %copy-start.7 = (f32[256,1,64]{2,1,0:T(1,128)S(1)}, f32[256,1,64]{2,1,0:T(1,128)}, u32[]{:S(2)}) copy-start(f32[256,1,64]{2,1,0:T(1,128)} %copy-done.6) | copy-start | bytes 196612
  129.3 13.0 %copy-start.10 = (f32[256,1,64]{2,1,0:T(1,128)S(1)}, f32[256,1,64]{2,1,0:T(1,128)}, u32[]{:S(2)}) copy-start(f32[256,1,64]{2,1,0:T(1,128)} %copy-done.9) | copy-start | bytes 196612
  132.8 23.1 %all-to-all-start.2 = ((f32[64,4,256]{2,1,0:T(4,128)}), f32[64,4,256]{2,1,0:T(4,128)S(1)}, u32[]{:S(2)}, u32[]{:S(2)}) async-start(f32[64,4,256]{2,1,0:T(4,128)} %all_to_all.84), calls=%async_computation.2 | async-start | bytes 524288 | tf_op jit(solution)/shard_map/all_to_all | solution.py:90
  (4 other events, 3.4 us)
where the time goes:
time: 158 us; the launch traced here: 157 us
  starting transfers between devices  76 us (48%)
  local copies, waits for them, and re-layouts  37.5 us (24%)
  waiting for transfers between devices  28.7 us (18%)
  other arithmetic  11.2 us (7%)
  between operations  3.48 us (2%)
    all_to_all x1, starting transfers between devices, per_device(): lax.all_to_all(volume.reshape(inl, columns), 'wide', split_axis=1, concat...  18.1 us
    all_to_all x1, starting transfers between devices, per_device(): lax.all_to_all(cond, 'narrow', split_axis=2, concat_axis=1, tiled=True)  13.6 us
    all_to_all x1, waiting for transfers between devices, per_device(): lax.all_to_all(solved, 'wide', split_axis=0, concat_axis=1, tiled=True)  12.3 us
    unnamed x116, local copies, waits for them, and re-layouts  10.2 us
    all_to_all x1, starting transfers between devices, per_device(): lax.all_to_all(solved, 'wide', split_axis=0, concat_axis=1, tiled=True)  9.56 us
    slice x69, local copies, waits for them, and re-layouts, halves(): return (paired[:, 0], paired[:, 1])  8.12 us
    all_to_all x1, waiting for transfers between devices, per_device(): lax.all_to_all(volume.reshape(inl, columns), 'wide', split_axis=1, concat...  7.98 us
    ppermute x2, starting transfers between devices, with_halo(): before = lax.ppermute(last, axis, up)  7.96 us
  transfers between devices with their start and end apart: 10, of which 5 were waited for; matrix products, arithmetic and copies ran while one was open for 28% of the time, Pallas kernels for 0%

commit v1 on v0

--- a/solution.py
+++ b/solution.py
@@ -81,8 +81,14 @@
     along_time = solved.T.reshape(inl, crs, tms)
     columns = crs * tms
     lines = (
-        lax.all_to_all(
-            volume.reshape(inl, columns), "wide", split_axis=1, concat_axis=0, tiled=True
+        jnp.concatenate(
+            lax.all_to_all(
+                jnp.stack(jnp.split(volume.reshape(inl, columns), lax.axis_size("wide"), axis=1)),
+                "wide",
+                0,
+                0,
+            ),
+            axis=0,
         ),
         lax.all_to_all(cond.reshape(inl, columns), "wide", split_axis=1, concat_axis=0, tiled=True),
     )

time: 158 us -> 199 us (1.26)
  local copies, waits for them, and re-layouts: 37.5 us -> 80.6 us
    unnamed x116 -> x182, local copies, waits for them, and re-layouts: 10.2 us -> 48.4 us
    all_to_all x1, waiting for transfers between devices: 7.98 us -> 0.01 us  [per_device(): lax.all_to_all(jnp.stack(jnp.split(volume.reshape(inl, columns), lax.axis...]
    all_to_all x1, starting transfers between devices: 7.28 us -> 14 us  [per_device(): lax.all_to_all(cond.reshape(inl, columns), 'wide', split_axis=1, concat_a...]
    all_to_all x1, waiting for transfers between devices: 0.01 us -> 6.33 us  [per_device(): lax.all_to_all(cond, 'narrow', split_axis=2, concat_axis=1, tiled=True)]
    all_to_all x1, starting transfers between devices: 7.79 us -> 3.41 us  [per_device(): lax.all_to_all(jnp.transpose(solved, (1, 0, 2)), 'narrow', split_axis=1,...]
    slice x69 -> x70, local copies, waits for them, and re-layouts: 8.12 us -> 8.77 us  [halves(): return (paired[:, 0], paired[:, 1])]
  transfers between devices with their start and end apart: 10 -> 10, of which waited for: 5 -> 5; matrix products, arithmetic and copies ran while one was open for 28% -> 43% of each run, Pallas kernels for 0% -> 0%
where the time goes in v1:
time: 199 us; the launch traced here: 198 us
  local copies, waits for them, and re-layouts  80.6 us (41%)
  starting transfers between devices  77.6 us (39%)
  waiting for transfers between devices  26.8 us (13%)
  other arithmetic  9.26 us (5%)
  between operations  3.48 us (2%)
    unnamed x182, local copies, waits for them, and re-layouts  48.4 us
    all_to_all x1, starting transfers between devices, per_device(): lax.all_to_all(jnp.stack(jnp.split(volume.reshape(inl, columns), lax.axis...  18.3 us
    all_to_all x1, starting transfers between devices, per_device(): lax.all_to_all(cond.reshape(inl, columns), 'wide', split_axis=1, concat_a...  14 us
    all_to_all x1, starting transfers between devices, per_device(): lax.all_to_all(cond, 'narrow', split_axis=2, concat_axis=1, tiled=True)  13.6 us
    all_to_all x1, waiting for transfers between devices, per_device(): lax.all_to_all(solved, 'wide', split_axis=0, concat_axis=1, tiled=True)  12.3 us
    slice x70, local copies, waits for them, and re-layouts, halves(): return (paired[:, 0], paired[:, 1])  8.77 us
    all_to_all x1, starting transfers between devices, per_device(): lax.all_to_all(solved, 'wide', split_axis=0, concat_axis=1, tiled=True)  8.49 us
    ppermute x2, starting transfers between devices, with_halo(): before = lax.ppermute(last, axis, up)  7.95 us
  transfers between devices with their start and end apart: 10, of which 5 were waited for; matrix products, arithmetic and copies ran while one was open for 43% of the time, Pallas kernels for 0%

profile of v1, /device:TPU:1, one launch (start us, length us, event | category | flops | bytes accessed | tf_op | source)
XLA Modules:
  0.0 197.7 jit_solution(7811611022381900841)
XLA Ops:
  0.0 1.5 fusion.175
  1.5 4.6 %collective-permute-start = (f32[1,16,1024]{2,1,0:T(8,128)S(1)}, f32[1,16,1024]{2,1,0:T(8,128)}, u32[]{:S(2)}, u32[]{:S(2)}) collective-permute-start(f32[1,16,1024]{2,1,0:T(8,128)S(1)} %get-tuple-element.81), channel_id=1, source_target_pairs={{0,8},{8,16},{16,24},{24,32},{32,40},{40,48},{48,56},{56,64},{64,7... | collective-permute-start | bytes 196616 | tf_op jit(solution)/shard_map/ppermute | solution.py:17
  6.1 6.2 %collective-permute-start.1 = (f32[1,16,1024]{2,1,0:T(8,128)}, f32[1,16,1024]{2,1,0:T(8,128)}, u32[]{:S(2)}, u32[]{:S(2)}) collective-permute-start(f32[1,16,1024]{2,1,0:T(8,128)} %get-tuple-element.80), channel_id=1, source_target_pairs={{8,0},{16,8},{24,16},{32,24},{40,32},{48,40},{56,48},{64,56},{72,6... | collective-permute-start | bytes 196616 | tf_op jit(solution)/shard_map/ppermute | solution.py:18
  12.3 1.7 copy.1454
  14.0 2.3 %reshape.942 = f32[8,1,8192]{2,1,0:T(1,128)} reshape(f32[1024,4,16]{2,1,0:T(4,128)S(1)} %bitcast.1843) | data formatting | bytes 524288
  16.3 4.4 %all-to-all-start.3 = ((f32[8,1,8192]{2,1,0:T(1,128)}), f32[8,1,8192]{2,1,0:T(1,128)S(1)}, u32[]{:S(2)}, u32[]{:S(2)}) async-start(f32[8,1,8192]{2,1,0:T(1,128)} %reshape.942), calls=%async_computation.3 | async-start | bytes 524288 | tf_op jit(solution)/shard_map/all_to_all | solution.py:100
  57.8 1.1 fusion.156
  61.2 3.4 %collective-permute-start.2 = (f32[6,1,1024]{2,1,0:T(1,128)S(1)}, f32[6,1,1024]{2,1,0:T(1,128)S(1)}, u32[]{:S(2)}, u32[]{:S(2)}) collective-permute-start(f32[6,1,1024]{2,1,0:T(1,128)S(1)} %get-tuple-element.38), channel_id=1, source_target_pairs={{0,1},{1,2},{2,3},{3,4},{4,5},{5,6},{6,7},{8,9},{9,10},{10,11},{11... | collective-permute-start | bytes 73736 | tf_op jit(solution)/shard_map/ppermute | solution.py:17
  64.6 1.3 collective-permute-start.3
  66.7 2.5 %collective-permute-done.3 = f32[6,1,1024]{2,1,0:T(1,128)S(1)} collective-permute-done((f32[6,1,1024]{2,1,0:T(1,128)S(1)}, f32[6,1,1024]{2,1,0:T(1,128)S(1)}, u32[]{:S(2)}, u32[]{:S(2)}) %collective-permute-start.3) | collective-permute-done | bytes 24608 | tf_op jit(solution)/shard_map/ppermute | solution.py:18
  70.4 1.1 fusion.157
  78.0 18.3 %all-to-all-start = ((f32[64,4,256]{2,1,0:T(4,128)}), f32[64,4,256]{2,1,0:T(4,128)}, u32[]{:S(2)}, u32[]{:S(2)}) async-start(f32[64,4,256]{2,1,0:T(4,128)} %constant_dynamic-update-slice_fusion), calls=%async_computation | async-start | bytes 524288 | tf_op jit(solution)/shard_map/all_to_all | solution.py:85
  98.6 2.3 %reshape.940 = f32[8,1,8192]{2,1,0:T(1,128)} reshape(f32[1024,4,16]{2,1,0:T(4,128)S(1)} %bitcast.1840) | data formatting | bytes 524288
  100.8 1.8 copy.1367
  105.1 2.1 %reduce.1 = f32[8,8192]{1,0:T(8,128)S(1)} reduce(f32[8,1,8192]{2,1,0:T(1,128)} %copy-done.14, f32[]{:T(128)} %broadcast.298), dimensions={1}, to_apply=%all_to_all.76.reduce_sub_computation | reduce | bytes 524292 | tf_op jit(solution)/shard_map/all_to_all | solution.py:100
  107.2 1.5 reshape.943
  110.2 13.6 %all-to-all-start.4 = ((f32[8,1,8192]{2,1,0:T(1,128)}), f32[8,1,8192]{2,1,0:T(1,128)S(1)}, u32[]{:S(2)}, u32[]{:S(2)}) async-start(f32[8,1,8192]{2,1,0:T(1,128)} %reshape.940), calls=%async_computation.4 | async-start | bytes 524288 | tf_op jit(solution)/shard_map/all_to_all | solution.py:101
  123.8 0.9 fusion.163
  124.7 1.2 reshape_reshape.3
  126.6 0.9 fusion.166
  127.5 6.3 %all-to-all-done.4 = f32[8,1,8192]{2,1,0:T(1,128)S(1)} async-done(((f32[8,1,8192]{2,1,0:T(1,128)}), f32[8,1,8192]{2,1,0:T(1,128)S(1)}, u32[]{:S(2)}, u32[]{:S(2)}) %all-to-all-start.4) | async-done | bytes 262176 | tf_op jit(solution)/shard_map/all_to_all | solution.py:101
  133.8 14.0 %all-to-all-start.1 = ((f32[4,64,256]{2,0,1:T(4,128)}), f32[4,64,256]{2,0,1:T(4,128)}, u32[]{:S(2)}, u32[]{:S(2)}) async-start(f32[4,64,256]{2,0,1:T(4,128)} %copy.1367), calls=%async_computation.1 | async-start | bytes 524288 | tf_op jit(solution)/shard_map/all_to_all | solution.py:93
  147.8 1.2 reduce
  149.0 1.5 reshape.941
  155.1 0.9 copy.1534
  156.0 5.3 %all-to-all-done.1 = f32[4,64,256]{2,0,1:T(4,128)} async-done(((f32[4,64,256]{2,0,1:T(4,128)}), f32[4,64,256]{2,0,1:T(4,128)}, u32[]{:S(2)}, u32[]{:S(2)}) %all-to-all-start.1) | async-done | bytes 262176 | tf_op jit(solution)/shard_map/all_to_all | solution.py:93
  161.3 3.4 %all-to-all-start.5 = ((f32[4,128,128]{2,0,1:T(4,128)}), f32[4,128,128]{2,0,1:T(4,128)S(1)}, u32[]{:S(2)}, u32[]{:S(2)}) async-start(f32[4,128,128]{2,0,1:T(4,128)} %copy.1534), calls=%async_computation.5 | async-start | bytes 524288 | tf_op jit(solution)/shard_map/all_to_all | solution.py:104
  164.7 1.0 all_to_all.72
  168.0 0.9 copy_bitcast_fusion.10
  173.4 0.9 all_to_all.73
  174.8 8.5 %all-to-all-start.2 = ((f32[64,4,256]{2,1,0:T(4,128)}), f32[64,4,256]{2,1,0:T(4,128)S(1)}, u32[]{:S(2)}, u32[]{:S(2)}) async-start(f32[64,4,256]{2,1,0:T(4,128)} %all_to_all.73), calls=%async_computation.2 | async-start | bytes 524288 | tf_op jit(solution)/shard_map/all_to_all | solution.py:96
  184.6 12.3 %all-to-all-done.2 = f32[64,4,256]{2,1,0:T(4,128)S(1)} async-done(((f32[64,4,256]{2,1,0:T(4,128)}), f32[64,4,256]{2,1,0:T(4,128)S(1)}, u32[]{:S(2)}, u32[]{:S(2)}) %all-to-all-start.2) | async-done | bytes 262176 | tf_op jit(solution)/shard_map/all_to_all | solution.py:96
  (540 shorter events, 65.5 us)
Async XLA Ops:
  1.5 58.0 %collective-permute-start = (f32[1,16,1024]{2,1,0:T(8,128)S(1)}, f32[1,16,1024]{2,1,0:T(8,128)}, u32[]{:S(2)}, u32[]{:S(2)}) collective-permute-start(f32[1,16,1024]{2,1,0:T(8,128)S(1)} %get-tuple-element.81), channel_id=1, source_target_pairs={{0,8},{8,16},{16,24},{24,32},{32,40},{40,48},{48,56},{56,64},{64,7... | collective-permute-start | bytes 196616 | tf_op jit(solution)/shard_map/ppermute | solution.py:17
  6.1 14.6 %copy-start = (f32[4,16,1024]{2,1,0:T(8,128)S(1)}, f32[4,16,1024]{2,1,0:T(8,128)}, u32[]{:S(2)}) copy-start(f32[4,16,1024]{2,1,0:T(8,128)} %param.1) | copy-start | bytes 786436
  6.1 54.2 %collective-permute-start.1 = (f32[1,16,1024]{2,1,0:T(8,128)}, f32[1,16,1024]{2,1,0:T(8,128)}, u32[]{:S(2)}, u32[]{:S(2)}) collective-permute-start(f32[1,16,1024]{2,1,0:T(8,128)} %get-tuple-element.80), channel_id=1, source_target_pairs={{8,0},{16,8},{24,16},{32,24},{40,32},{48,40},{56,48},{64,56},{72,6... | collective-permute-start | bytes 196616 | tf_op jit(solution)/shard_map/ppermute | solution.py:18
  16.3 61.7 %all-to-all-start.3 = ((f32[8,1,8192]{2,1,0:T(1,128)}), f32[8,1,8192]{2,1,0:T(1,128)S(1)}, u32[]{:S(2)}, u32[]{:S(2)}) async-start(f32[8,1,8192]{2,1,0:T(1,128)} %reshape.942), calls=%async_computation.3 | async-start | bytes 524288 | tf_op jit(solution)/shard_map/all_to_all | solution.py:100
  61.2 5.5 %collective-permute-start.2 = (f32[6,1,1024]{2,1,0:T(1,128)S(1)}, f32[6,1,1024]{2,1,0:T(1,128)S(1)}, u32[]{:S(2)}, u32[]{:S(2)}) collective-permute-start(f32[6,1,1024]{2,1,0:T(1,128)S(1)} %get-tuple-element.38), channel_id=1, source_target_pairs={{0,1},{1,2},{2,3},{3,4},{4,5},{5,6},{6,7},{8,9},{9,10},{10,11},{11... | collective-permute-start | bytes 73736 | tf_op jit(solution)/shard_map/ppermute | solution.py:17
  64.6 4.6 %collective-permute-start.3 = (f32[6,1,1024]{2,1,0:T(1,128)S(1)}, f32[6,1,1024]{2,1,0:T(1,128)S(1)}, u32[]{:S(2)}, u32[]{:S(2)}) collective-permute-start(f32[6,1,1024]{2,1,0:T(1,128)S(1)} %get-tuple-element.39), channel_id=1, source_target_pairs={{1,0},{2,1},{3,2},{4,3},{5,4},{6,5},{7,6},{9,8},{10,9},{11,10},{12... | collective-permute-start | bytes 73736 | tf_op jit(solution)/shard_map/ppermute | solution.py:18
  72.5 1.0 copy-start.11
  73.9 1.2 copy-start.2
  75.4 1.1 copy-start.15
  75.5 1.0 copy-start.12
  78.0 18.3 %copy-start.22 = (f32[32,2,64]{2,1,0:T(2,128)}, f32[32,2,64]{2,1,0:T(2,128)S(1)}, u32[]{:S(2)}) copy-start(f32[32,2,64]{2,1,0:T(2,128)S(1)} %copy.1640) | copy-start | bytes 49156
  78.0 18.3 %copy-start.14 = (f32[8,1,8192]{2,1,0:T(1,128)}, f32[8,1,8192]{2,1,0:T(1,128)S(1)}, u32[]{:S(2)}) copy-start(f32[8,1,8192]{2,1,0:T(1,128)S(1)} %all-to-all-done.3) | copy-start | bytes 786436
  78.0 32.2 %all-to-all-start = ((f32[64,4,256]{2,1,0:T(4,128)}), f32[64,4,256]{2,1,0:T(4,128)}, u32[]{:S(2)}, u32[]{:S(2)}) async-start(f32[64,4,256]{2,1,0:T(4,128)} %constant_dynamic-update-slice_fusion), calls=%async_computation | async-start | bytes 524288 | tf_op jit(solution)/shard_map/all_to_all | solution.py:85
  98.6 4.1 %copy-start.23 = (f32[32,2,64]{2,1,0:T(2,128)S(1)}, f32[32,2,64]{2,1,0:T(2,128)}, u32[]{:S(2)}) copy-start(f32[32,2,64]{2,1,0:T(2,128)} %copy-done.22) | copy-start | bytes 49156
  98.6 4.1 %copy-start.26 = (f32[64,1,64]{2,0,1:T(8,128)S(1)}, f32[64,1,64]{2,0,1:T(8,128)}, u32[]{:S(2)}) copy-start(f32[64,1,64]{2,0,1:T(8,128)} %divide_bitcast_fusion.2) | copy-start | bytes 49156
  98.6 4.2 %copy-start.13 = (f32[128,1,64]{2,1,0:T(1,128)S(1)}, f32[128,1,64]{2,1,0:T(1,128)}, u32[]{:S(2)}) copy-start(f32[128,1,64]{2,1,0:T(1,128)} %copy-done.12) | copy-start | bytes 98308
  98.6 4.2 %copy-start.16 = (f32[128,1,64]{2,1,0:T(1,128)S(1)}, f32[128,1,64]{2,1,0:T(1,128)}, u32[]{:S(2)}) copy-start(f32[128,1,64]{2,1,0:T(1,128)} %copy-done.15) | copy-start | bytes 98308
  98.6 4.2 %copy-start.18 = (f32[128,1,64]{2,1,0:T(1,128)S(1)}, f32[128,1,64]{2,1,0:T(1,128)}, u32[]{:S(2)}) copy-start(f32[128,1,64]{2,1,0:T(1,128)} %copy-done.17) | copy-start | bytes 98308
  110.2 23.6 %all-to-all-start.4 = ((f32[8,1,8192]{2,1,0:T(1,128)}), f32[8,1,8192]{2,1,0:T(1,128)S(1)}, u32[]{:S(2)}, u32[]{:S(2)}) async-start(f32[8,1,8192]{2,1,0:T(1,128)} %reshape.940), calls=%async_computation.4 | async-start | bytes 524288 | tf_op jit(solution)/shard_map/all_to_all | solution.py:101
  133.8 27.5 %all-to-all-start.1 = ((f32[4,64,256]{2,0,1:T(4,128)}), f32[4,64,256]{2,0,1:T(4,128)}, u32[]{:S(2)}, u32[]{:S(2)}) async-start(f32[4,64,256]{2,0,1:T(4,128)} %copy.1367), calls=%async_computation.1 | async-start | bytes 524288 | tf_op jit(solution)/shard_map/all_to_all | solution.py:93
  151.3 1.1 copy-start.25
  151.3 1.2 copy-start.7
  151.4 1.2 copy-start.21
  161.3 13.5 %all-to-all-start.5 = ((f32[4,128,128]{2,0,1:T(4,128)}), f32[4,128,128]{2,0,1:T(4,128)S(1)}, u32[]{:S(2)}, u32[]{:S(2)}) async-start(f32[4,128,128]{2,0,1:T(4,128)} %copy.1534), calls=%async_computation.5 | async-start | bytes 524288 | tf_op jit(solution)/shard_map/all_to_all | solution.py:104
  165.9 2.1 %copy-start.24 = (f32[127,1,256]{2,1,0:T(1,128)S(1)}, f32[127,1,256]{2,1,0:T(1,128)}, u32[]{:S(2)}) copy-start(f32[127,1,256]{2,1,0:T(1,128)} %slice.1816) | copy-start | bytes 390148
  166.1 2.8 %copy-start.6 = (f32[128,1,256]{2,1,0:T(1,128)S(1)}, f32[128,1,256]{2,1,0:T(1,128)}, u32[]{:S(2)}) copy-start(f32[128,1,256]{2,1,0:T(1,128)} %get-tuple-element.58) | copy-start | bytes 393220
  166.1 2.8 %copy-start.20 = (f32[128,1,256]{2,1,0:T(1,128)S(1)}, f32[128,1,256]{2,1,0:T(1,128)}, u32[]{:S(2)}) copy-start(f32[128,1,256]{2,1,0:T(1,128)} %get-tuple-element.59) | copy-start | bytes 393220
  172.7 10.6 %copy-start.1 = (f32[128,2,64]{2,1,0:T(2,128)S(1)}, f32[128,2,64]{2,1,0:T(2,128)}, u32[]{:S(2)}) copy-start(f32[128,2,64]{2,1,0:T(2,128)} %copy.1646) | copy-start | bytes 196612
  172.7 10.6 %copy-start.3 = (f32[256,1,64]{2,1,0:T(1,128)S(1)}, f32[256,1,64]{2,1,0:T(1,128)}, u32[]{:S(2)}) copy-start(f32[256,1,64]{2,1,0:T(1,128)} %copy-done.2) | copy-start | bytes 196612
  172.7 10.6 %copy-start.5 = (f32[256,1,64]{2,1,0:T(1,128)S(1)}, f32[256,1,64]{2,1,0:T(1,128)}, u32[]{:S(2)}) copy-start(f32[256,1,64]{2,1,0:T(1,128)} %copy-done.4) | copy-start | bytes 196612
  172.8 10.6 %copy-start.9 = (f32[256,1,64]{2,1,0:T(1,128)S(1)}, f32[256,1,64]{2,1,0:T(1,128)}, u32[]{:S(2)}) copy-start(f32[256,1,64]{2,1,0:T(1,128)} %copy-done.8) | copy-start | bytes 196612
  174.8 22.0 %all-to-all-start.2 = ((f32[64,4,256]{2,1,0:T(4,128)}), f32[64,4,256]{2,1,0:T(4,128)S(1)}, u32[]{:S(2)}, u32[]{:S(2)}) async-start(f32[64,4,256]{2,1,0:T(4,128)} %all_to_all.73), calls=%async_computation.2 | async-start | bytes 524288 | tf_op jit(solution)/shard_map/all_to_all | solution.py:96
  (5 other events, 4.4 us)
